TPU v7x, 256 devices: a whole 4x4x8 slice. The times are simulated.
256 devices in a mesh: tm: 32 (over y, z), head: 8 (over x, core).
Axes of the slice: x: 4, y: 4, z: 8, core: 2. Of those that a mesh axis runs over, the one named last changes fastest.
Arguments:
- query: bfloat16 [6144, 3072], P(('tm', 'head')), may hold values from -6 to 6
- keys: bfloat16 [6144, 3072], P(('tm', 'head')), may hold values from -6 to 6
- values: bfloat16 [6144, 3072], P(('tm', 'head')), may hold values from -6 to 6
- dout: bfloat16 [6144, 3072], P(('tm', 'head')), may hold values from -6 to 6
- slot_group: int32 [32], replicated, may hold values from 0 to 31, each once
- valid: int32 [32], replicated, may hold values from 48 to 192, as said below
Outputs:
- grad_query: bfloat16 [6144, 3072], P(('tm', 'head'))
- grad_keys: bfloat16 [6144, 3072], P(('tm', 'head'))
- grad_values: bfloat16 [6144, 3072], P(('tm', 'head'))
Inputs may be any that keep to these rules, and one draw needn't show every extreme that they name: `slot_group`: each group number appears once. valid tokens are the first of each group; some group is full.
All inputs are finite; a program needn't handle non-finite values.
Results may differ from a plain program's by a relative error of at most 0.015.
Values may be sent and summed in bfloat16 or wider, within the bound.
No kernel may reach another device: no remote copies, remote signals or barrier semaphores. Data moves between devices by JAX's collectives and lax.ppermute only.
A program may use at most 64 MiB of HBM per device.

v0:
```python
import math

import jax
import jax.numpy as jnp
from jax import lax
from jax.sharding import PartitionSpec as P

HD = 128


NEG_FILL = -1e30


def in_blocks(update, carry, piece, shard_rows):
    piece_rows = piece[0].shape[0]
    limit_rows = shard_rows * -(-512 // shard_rows)
    block_rows = math.gcd(piece_rows, limit_rows)
    block_count = piece_rows // block_rows
    stacked = tuple(
        (member.reshape((block_count, block_rows) + member.shape[1:]) for member in piece)
    )

    def one_block(state, inputs):
        block_index, members = inputs
        return (update(state, members, block_index * block_rows), None)

    carry, _ = lax.scan(one_block, carry, (jnp.arange(block_count, dtype=jnp.int32), stacked))
    return carry


def local(query, keys, values, dout, slot_group, valid):
    scale = 1.0 / math.sqrt(HD)
    query, keys, values, dout = (
        lax.all_to_all(query, "head", split_axis=1, concat_axis=0, tiled=True),
        lax.all_to_all(keys, "head", split_axis=1, concat_axis=0, tiled=True),
        lax.all_to_all(values, "head", split_axis=1, concat_axis=0, tiled=True),
        lax.all_to_all(dout, "head", split_axis=1, concat_axis=0, tiled=True),
    )
    shard_rows = query.shape[0]
    head_count = query.shape[1] // HD
    slot_total = slot_group.shape[0]
    slot_numbers = jnp.arange(slot_total, dtype=jnp.int32)
    my_slot = lax.axis_index("tm")
    my_group = jnp.sum(jnp.where(slot_numbers == my_slot, slot_group, 0))
    my_valid = jnp.sum(jnp.where(slot_numbers == my_group, valid, 0))
    my_live = jnp.arange(shard_rows, dtype=jnp.int32) < my_valid
    masked_dout = jnp.where(my_live[:, None], dout, jnp.zeros_like(dout))
    query_heads = query.reshape(shard_rows, head_count, HD)
    key_heads = keys.reshape(shard_rows, head_count, HD)
    value_heads = values.reshape(shard_rows, head_count, HD)
    grad_heads = masked_dout.reshape(shard_rows, head_count, HD)

    def piece_groups(start, count):
        token_index = start + jnp.arange(count, dtype=jnp.int32)
        piece_slot = token_index // shard_rows
        piece_group = jnp.sum(
            jnp.where(piece_slot[:, None] == slot_numbers[None, :], slot_group[None, :], 0), axis=1
        )
        group_valid = jnp.sum(
            jnp.where(piece_group[:, None] == slot_numbers[None, :], valid[None, :], 0), axis=1
        )
        return (piece_group, token_index % shard_rows < group_valid)

    def key_allowed(start, count):
        piece_group, piece_live = piece_groups(start, count)
        return piece_live & (piece_group <= my_group)

    def forward_update(carry, piece, start):
        piece_keys, piece_values = piece
        count = piece_keys.shape[0]
        allowed = key_allowed(start, count)
        row_top, total, summed = carry
        scores = (
            jnp.einsum(
                "qhd,khd->hqk",
                query_heads,
                piece_keys.reshape(count, head_count, HD),
                preferred_element_type=jnp.float32,
            )
            * scale
        )
        scores = jnp.where(allowed[None, None, :], scores, NEG_FILL)
        new_top = jnp.maximum(row_top, jnp.max(scores, axis=2))
        weights = jnp.where(allowed[None, None, :], jnp.exp(scores - new_top[:, :, None]), 0.0)
        factor = jnp.exp(row_top - new_top)
        total = total * factor + jnp.sum(weights, axis=2)
        summed = summed * factor[:, :, None] + jnp.einsum(
            "hqk,khd->hqd",
            weights.astype(jnp.bfloat16),
            piece_values.reshape(count, head_count, HD),
            preferred_element_type=jnp.float32,
        )
        return (new_top, total, summed)

    forward_init = (
        jnp.full((head_count, shard_rows), NEG_FILL, jnp.float32),
        jnp.zeros((head_count, shard_rows), jnp.float32),
        jnp.zeros((head_count, shard_rows, HD), jnp.float32),
    )
    row_top, total, summed = in_blocks(
        forward_update,
        forward_init,
        (
            lax.all_gather(keys, "tm", axis=0, tiled=True),
            lax.all_gather(values, "tm", axis=0, tiled=True),
        ),
        shard_rows,
    )
    attended = summed / total[:, :, None]
    log_total = row_top + jnp.log(total)
    delta = jnp.einsum("qhd,hqd->hq", grad_heads.astype(jnp.float32), attended)
    all_log_total, all_delta = (
        lax.all_gather(log_total.T, "tm", axis=0, tiled=True),
        lax.all_gather(delta.T, "tm", axis=0, tiled=True),
    )

    def query_update(carry, piece, start):
        piece_keys, piece_values = piece
        count = piece_keys.shape[0]
        allowed = key_allowed(start, count)
        piece_key_heads = piece_keys.reshape(count, head_count, HD)
        scores = (
            jnp.einsum(
                "qhd,khd->hqk", query_heads, piece_key_heads, preferred_element_type=jnp.float32
            )
            * scale
        )
        scores = jnp.where(allowed[None, None, :], scores, NEG_FILL)
        probs = jnp.where(allowed[None, None, :], jnp.exp(scores - log_total[:, :, None]), 0.0)
        dprobs = jnp.einsum(
            "qhd,khd->hqk",
            grad_heads,
            piece_values.reshape(count, head_count, HD),
            preferred_element_type=jnp.float32,
        )
        dscores = (probs * (dprobs - delta[:, :, None]) * scale).astype(jnp.bfloat16)
        return carry + jnp.einsum(
            "hqk,khd->hqd", dscores, piece_key_heads, preferred_element_type=jnp.float32
        )

    def keyside_update(carry, piece, start):
        piece_query, piece_grad = piece
        count = piece_query.shape[0]
        piece_group, piece_live = piece_groups(start, count)
        allowed = (piece_group[:, None] >= my_group) & my_live[None, :]
        piece_log = lax.dynamic_slice_in_dim(all_log_total, start, count, 0).T
        piece_delta = lax.dynamic_slice_in_dim(all_delta, start, count, 0).T
        key_grad, value_grad = carry
        piece_query_heads = piece_query.reshape(count, head_count, HD)
        piece_grad_heads = piece_grad.reshape(count, head_count, HD)
        scores = (
            jnp.einsum(
                "qhd,khd->hqk", piece_query_heads, key_heads, preferred_element_type=jnp.float32
            )
            * scale
        )
        scores = jnp.where(allowed[None, :, :], scores, NEG_FILL)
        probs = jnp.where(allowed[None, :, :], jnp.exp(scores - piece_log[:, :, None]), 0.0)
        dprobs = jnp.einsum(
            "qhd,khd->hqk", piece_grad_heads, value_heads, preferred_element_type=jnp.float32
        )
        dscores = (probs * (dprobs - piece_delta[:, :, None]) * scale).astype(jnp.bfloat16)
        key_grad = key_grad + jnp.einsum(
            "hqk,qhd->khd", dscores, piece_query_heads, preferred_element_type=jnp.float32
        )
        value_grad = value_grad + jnp.einsum(
            "hqk,qhd->khd",
            probs.astype(jnp.bfloat16),
            piece_grad_heads,
            preferred_element_type=jnp.float32,
        )
        return (key_grad, value_grad)

    query_init = jnp.zeros((head_count, shard_rows, HD), jnp.float32)
    keyside_init = (
        jnp.zeros((shard_rows, head_count, HD), jnp.float32),
        jnp.zeros((shard_rows, head_count, HD), jnp.float32),
    )
    query_grad = in_blocks(
        query_update,
        query_init,
        (
            lax.all_gather(keys, "tm", axis=0, tiled=True),
            lax.all_gather(values, "tm", axis=0, tiled=True),
        ),
        shard_rows,
    )
    key_grad, value_grad = in_blocks(
        keyside_update,
        keyside_init,
        (
            lax.all_gather(query, "tm", axis=0, tiled=True),
            lax.all_gather(masked_dout, "tm", axis=0, tiled=True),
        ),
        shard_rows,
    )
    query_out = (
        query_grad.transpose(1, 0, 2).reshape(shard_rows, head_count * HD).astype(jnp.bfloat16)
    )
    key_out = key_grad.reshape(shard_rows, head_count * HD).astype(jnp.bfloat16)
    value_out = value_grad.reshape(shard_rows, head_count * HD).astype(jnp.bfloat16)
    return (
        lax.all_to_all(query_out, "head", split_axis=0, concat_axis=1, tiled=True),
        lax.all_to_all(key_out, "head", split_axis=0, concat_axis=1, tiled=True),
        lax.all_to_all(value_out, "head", split_axis=0, concat_axis=1, tiled=True),
    )


def solution(mesh):
    in_specs = (
        P(("tm", "head"), None),
        P(("tm", "head"), None),
        P(("tm", "head"), None),
        P(("tm", "head"), None),
        P(),
        P(),
    )
    out_specs = (P(("tm", "head"), None), P(("tm", "head"), None), P(("tm", "head"), None))
    return jax.shard_map(local, mesh=mesh, in_specs=in_specs, out_specs=out_specs, check_vma=False)
```

profile of v0, /device:TPU:1, one launch (start us, length us, event | category | flops | bytes accessed | tf_op | source)
XLA Modules:
  0.0 733.9 jit_solution(4757219695729062643)
XLA Ops:
  8.2 11.7 %all_to_all.127 = bf16[24,8,384]{2,0,1:T(8,128)(2,1)} all-to-all(bf16[24,8,384]{2,0,1:T(8,128)(2,1)S(1)} %bitcast.110), channel_id=1, replica_groups=mesh['tm'=32,'head'=8] {'head'}, dimensions={1} | all-to-all | bytes 294912 | tf_op jit(solution)/shard_map/all_to_all | solution.py:35
  20.9 9.4 %all_to_all.128 = bf16[24,8,384]{2,0,1:T(8,128)(2,1)} all-to-all(bf16[24,8,384]{2,0,1:T(8,128)(2,1)S(1)} %bitcast.111), channel_id=1, replica_groups=mesh['tm'=32,'head'=8] {'head'}, dimensions={1} | all-to-all | bytes 294912 | tf_op jit(solution)/shard_map/all_to_all | solution.py:36
  31.3 9.4 %all_to_all.129 = bf16[24,8,384]{2,0,1:T(8,128)(2,1)} all-to-all(bf16[24,8,384]{2,0,1:T(8,128)(2,1)S(1)} %bitcast.112), channel_id=1, replica_groups=mesh['tm'=32,'head'=8] {'head'}, dimensions={1} | all-to-all | bytes 294912 | tf_op jit(solution)/shard_map/all_to_all | solution.py:34
  40.7 1.6 copy.200
  42.2 4.2 all-to-all-start.3
  46.4 1.3 fusion.54
  47.7 1.9 fusion.55
  55.0 46.6 %all-gather.7.cloned.1.call-done = bf16[6144,384]{1,0:T(8,128)(2,1)} async-done(((bf16[192,384]{1,0:T(8,128)(2,1)}), bf16[6144,384]{1,0:T(8,128)(2,1)}) %all-gather.7.cloned.1.call-update) | async-done | bytes 4718608 | tf_op jit(solution)/shard_map/all_gather | solution.py:183
  101.6 83.4 %all-gather.9.cloned.1.call-done = bf16[6144,384]{1,0:T(8,128)(2,1)} async-done(((bf16[192,384]{1,0:T(8,128)(2,1)}), bf16[6144,384]{1,0:T(8,128)(2,1)}) %all-gather.9.cloned.1.call-update) | async-done | bytes 4718608 | tf_op jit(solution)/shard_map/all_gather | solution.py:184
  185.0 132.0 %while.51 = (s32[]{:T(128)}, f32[3,192]{1,0:T(4,128)S(1)}, f32[3,192]{1,0:T(4,128)S(1)}, f32[3,192,128]{2,1,0:T(8,128)S(1)}, s32[32]{0:T(128)S(1)}, /*index=5*/s...) while((s32[]{:T(128)}, f32[3,192]{1,0:T(4,128)S(1)}, ...), condition=%wide.region_6.7_spmd.clone.clone, body=%wide.region_1.6_spmd.clone.clone.sunk | while | flops 57882628 | bytes 3582657 | solution.py:27
  317.3 130.6 %while.52 = (s32[]{:T(128)}, f32[3,192,128]{2,1,0:T(8,128)S(1)}, s32[32]{0:T(128)S(1)}, s32[32]{0:T(128)S(1)}, s32[32]{0:T(128)S(1)}, /*index=5*/s32[]{:T(128)},...) while((s32[]{:T(128)}, f32[3,192,128]{2,1,0:T(8,128)S(1)}, ...), condition=%wide.region_11.12_spmd.clone.clone, body=%wide.region_8.11_spmd.clone.clone.sunk | while | flops 86006976 | bytes 3402567 | solution.py:27
  448.9 8.0 %all-to-all-start.4 = ((bf16[8,24,384]{2,1,0:T(8,128)(2,1)}), bf16[8,24,384]{2,1,0:T(8,128)(2,1)S(1)}, u32[]{:S(2)}, u32[]{:S(2)}) async-start(bf16[8,24,384]{2,1,0:T(8,128)(2,1)} %convert_element_type.55), calls=%async_computation.4 | async-start | bytes 294912 | tf_op jit(solution)/shard_map/all_to_all | solution.py:203
  456.9 32.1 %all-gather = f32[32,192,3]{1,2,0:T(4,128)S(1)} all-gather(f32[1,192,3]{1,2,0:T(4,128)S(1)} %bitcast.125), channel_id=1, replica_groups=mesh['tm'=32,'head'=8] {'tm'}, dimensions={0}, use_global_device_ids=true | all-gather | bytes 76032 | tf_op jit(solution)/shard_map/all_gather | solution.py:113
  489.1 30.9 %all-gather.1 = f32[32,192,3]{1,2,0:T(4,128)S(1)} all-gather(f32[1,192,3]{1,2,0:T(4,128)S(1)} %bitcast.115), channel_id=1, replica_groups=mesh['tm'=32,'head'=8] {'tm'}, dimensions={0}, use_global_device_ids=true | all-gather | bytes 76032 | tf_op jit(solution)/shard_map/all_gather | solution.py:114
  520.2 165.6 %while.53 = (s32[]{:T(128)}, f32[192,3,128]{2,0,1:T(8,128)S(1)}, f32[192,3,128]{2,0,1:T(8,128)S(1)}, bf16[32,192,384]{2,1,0:T(8,128)(2,1)}, s32[32]{0:T(128)S(1)...) while((s32[]{:T(128)}, f32[192,3,128]{2,0,1:T(8,128)S(1)}, ...), condition=%wide.region_14.15_spmd.clone.clone, body=%wide.region_12.14_spmd.clone.clone.sunk | while | flops 114593664 | bytes 4663038 | solution.py:27
  532.0 1.2 iota_compare_fusion.3
  547.5 1.2 iota_compare_fusion.3
  563.0 1.2 iota_compare_fusion.3
  578.6 1.2 iota_compare_fusion.3
  588.9 1.2 iota_compare_fusion.3
  686.8 24.9 %all-to-all-start.5 = ((bf16[8,24,384]{2,1,0:T(8,128)(2,1)}), bf16[8,24,384]{2,1,0:T(8,128)(2,1)S(1)}, u32[]{:S(2)}, u32[]{:S(2)}) async-start(bf16[8,24,384]{2,1,0:T(8,128)(2,1)} %convert_element_type.57), calls=%async_computation.5 | async-start | bytes 294912 | tf_op jit(solution)/shard_map/all_to_all | solution.py:204
  712.6 4.5 all-to-all-done.5
  717.1 4.2 all-to-all-start.6
  722.6 4.1 all-to-all-done.6
  (1204 shorter events, 367.0 us)
Async XLA Ops:
  7.2 177.8 %copy-start = (s32[32]{0:T(128)S(1)}, s32[32]{0:T(128)}, u32[]{:S(2)}) copy-start(s32[32]{0:T(128)} %param.16) | copy-start | bytes 388
  7.2 177.8 %copy-start.1 = (s32[32]{0:T(128)S(1)}, s32[32]{0:T(128)}, u32[]{:S(2)}) copy-start(s32[32]{0:T(128)} %param.17) | copy-start | bytes 388
  7.2 94.4 %all-gather.7.cloned.1.call-start = ((), (), s32[]{:S(2)}) async-start(), calls=%async_computation.7 | async-start | bytes 4866048 | tf_op jit(solution)/shard_map/all_gather | solution.py:183
  19.9 165.1 %all-gather.9.cloned.1.call-start = ((), (), s32[]{:S(2)}) async-start(), calls=%async_computation.8 | async-start | bytes 4866048 | tf_op jit(solution)/shard_map/all_gather | solution.py:184
  30.3 489.9 %all-gather.11.cloned.1.call-start = ((), (), s32[]{:S(2)}) async-start(), calls=%async_computation.9 | async-start | bytes 4866048 | tf_op jit(solution)/shard_map/all_gather | solution.py:192
  42.2 9.6 %all-to-all-start.3 = ((bf16[24,8,384]{2,0,1:T(8,128)(2,1)}), bf16[24,8,384]{2,0,1:T(8,128)(2,1)S(1)}, u32[]{:S(2)}, u32[]{:S(2)}) async-start(bf16[24,8,384]{2,0,1:T(8,128)(2,1)} %bitcast.74), calls=%async_computation.3 | async-start | bytes 294912 | tf_op jit(solution)/shard_map/all_to_all | solution.py:37
  46.4 473.8 %all-gather.13.cloned.1.call-start = ((), (), s32[]{:S(2)}) async-start(), calls=%async_computation.10 | async-start | bytes 4866048 | tf_op jit(solution)/shard_map/all_gather | solution.py:193
  448.9 237.8 %all-to-all-start.4 = ((bf16[8,24,384]{2,1,0:T(8,128)(2,1)}), bf16[8,24,384]{2,1,0:T(8,128)(2,1)S(1)}, u32[]{:S(2)}, u32[]{:S(2)}) async-start(bf16[8,24,384]{2,1,0:T(8,128)(2,1)} %convert_element_type.55), calls=%async_computation.4 | async-start | bytes 294912 | tf_op jit(solution)/shard_map/all_to_all | solution.py:203
  686.8 30.4 %all-to-all-start.5 = ((bf16[8,24,384]{2,1,0:T(8,128)(2,1)}), bf16[8,24,384]{2,1,0:T(8,128)(2,1)S(1)}, u32[]{:S(2)}, u32[]{:S(2)}) async-start(bf16[8,24,384]{2,1,0:T(8,128)(2,1)} %convert_element_type.57), calls=%async_computation.5 | async-start | bytes 294912 | tf_op jit(solution)/shard_map/all_to_all | solution.py:204
  717.1 9.6 %all-to-all-start.6 = ((bf16[8,24,384]{2,1,0:T(8,128)(2,1)}), bf16[8,24,384]{2,1,0:T(8,128)(2,1)S(1)}, u32[]{:S(2)}, u32[]{:S(2)}) async-start(bf16[8,24,384]{2,1,0:T(8,128)(2,1)} %convert_element_type.59), calls=%async_computation.6 | async-start | bytes 294912 | tf_op jit(solution)/shard_map/all_to_all | solution.py:205
Sparse Core Ops, SparseCore 0:
  20.0 81.5 all-gather.6
  104.2 80.7 all-gather.8
  187.6 80.9 all-gather.10
  271.6 80.7 all-gather.12
where the time goes:
time: 739 us; the launch traced here: 734 us
  local copies, waits for them, and re-layouts  178 us (24%)
  waiting for transfers between devices  139 us (19%)
  other arithmetic  105 us (14%)
  matrix products  93.6 us (13%)
  blocking collectives  93.4 us (13%)
  loops' own time  68.9 us (9%)
  starting transfers between devices  41.3 us (6%)
  between operations  14 us (2%)
    dynamic_slice x192, local copies, waits for them, and re-layouts, in_blocks(): lax.scan(one_block, carry, (jnp.arange(block_count, dtype=jnp.int32), sta...  154 us
    all_gather x1, waiting for transfers between devices, local(): lax.all_gather(values, 'tm', axis=0, tiled=True)  83.4 us
    another operation x3, loops' own time, in_blocks(): lax.scan(one_block, carry, (jnp.arange(block_count, dtype=jnp.int32), sta...  68.9 us
    all_gather x1, waiting for transfers between devices, local(): lax.all_gather(keys, 'tm', axis=0, tiled=True)  46.6 us
    lt x33, other arithmetic, local(): my_live = jnp.arange(shard_rows, dtype=jnp.int32) < my_valid  39 us
    and x64, other arithmetic, key_allowed(): return piece_live & (piece_group <= my_group)  36.8 us
    all_gather x1, blocking collectives, local(): lax.all_gather(log_total.T, 'tm', axis=0, tiled=True)  32.1 us
    all_gather x1, blocking collectives, local(): lax.all_gather(delta.T, 'tm', axis=0, tiled=True)  30.9 us
  transfers between devices with their start and end apart: 8, of which 5 were waited for; matrix products, arithmetic and copies ran while one was open for 51% of the time, Pallas kernels for 0%

commit v1 on v0

v1 whole, which is shorter than its diff:
```python
import functools
import math

import jax
import jax.numpy as jnp
from jax import lax
from jax.experimental import pallas as pl
from jax.experimental.pallas import tpu as pltpu
from jax.sharding import PartitionSpec as P

HD = 128
HEADS = 3
COLS = HEADS * HD
NY, NZ, NX, NC = 4, 8, 4, 2
PART = 48
SUB = 24
GROUP = 192
QROWS = 768
NEG = -1e30
SCALE = 1.0 / math.sqrt(HD)
LOG2E = 1.4426950408889634
QCHUNK = 256

NT = (((1,), (1,)), ((), ()))
NN = (((1,), (0,)), ((), ()))
TN = (((0,), (0,)), ((), ()))


def pairs(move):
    out = []
    for y in range(NY):
        for z in range(NZ):
            for x in range(NX):
                for c in range(NC):
                    ty, tz, tx, tc = move(y, z, x, c)
                    ty, tz, tx = ty % NY, tz % NZ, tx % NX
                    out.append((((y * NZ + z) * NX + x) * NC + c, ((ty * NZ + tz) * NX + tx) * NC + tc))
    return out


def send(array, move):
    return lax.ppermute(array, ("tm", "head"), pairs(move))


def swap_core(array):
    return send(array, lambda y, z, x, c: (y, z, x, 1 - c))


def dot(a, b, dims):
    return lax.dot_general(a, b, dims, preferred_element_type=jnp.float32)


def row_positions(part):
    row = lax.broadcasted_iota(jnp.int32, (GROUP, QCHUNK), 0)
    piece = row // PART
    return PART * ((part - piece) & 3) + (row - PART * piece)


def pack_kernel(at, query, grad, keys, values, keep, give):
    z, c = at[1], at[3]
    for j in range(4):
        mine = pl.ds(pl.multiple_of(((z + c + 2 * j) & 7) * COLS, HD), COLS)
        theirs = pl.ds(pl.multiple_of(((z + 1 - c + 2 * j) & 7) * COLS, HD), COLS)
        for n, array in enumerate((query, grad, keys, values)):
            keep[j, n] = array[:, mine]
            give[j, n] = array[:, theirs]


def unpack_kernel(at, mine, theirs, *outs):
    z, c = at[1], at[3]
    for j in range(4):
        own = pl.ds(pl.multiple_of(((z + c + 2 * j) & 7) * COLS, HD), COLS)
        other = pl.ds(pl.multiple_of(((z + 1 - c + 2 * j) & 7) * COLS, HD), COLS)
        for n in range(3):
            outs[n][:, own] = mine[j, n]
            outs[n][:, other] = theirs[j, n]


def query_slot(at, s, j):
    return ((at[0] - s) & 3) * NZ + ((at[1] - at[3] - 2 * j) & 7)


def key_slot(at, ks):
    o = ks // 4
    core = at[3] + o - 2 * o * at[3]
    return at[0] * NZ + ((at[1] - core - 2 * (ks - 4 * o)) & 7)


def query_groups(at, groups):
    lane = lax.broadcasted_iota(jnp.int32, (1, QROWS), 1)
    out = jnp.zeros((1, QROWS), jnp.int32)
    for s in range(4):
        for j in range(4):
            out = jnp.where(lane >= (s * 4 + j) * PART, groups[query_slot(at, s, j)], out)
    return out


def stats_kernel(at, groups, valid, *refs):
    qd = refs[0:4]
    kv = refs[4:12]
    qbuf, kbuf, stats, pos_ref = refs[12:16]
    part = at[2]
    row = lax.broadcasted_iota(jnp.int32, (PART, COLS), 0) + part * PART
    for s in range(4):
        for j in range(4):
            rows = pl.ds((s * 4 + j) * PART, PART)
            live = row < valid[groups[query_slot(at, s, j)]]
            qbuf[0, rows, :] = qd[s][j, 0]
            grad = qd[s][j, 1]
            qbuf[1, rows, :] = jnp.where(live, grad, jnp.zeros_like(grad))
    for o in range(2):
        for s in range(4):
            for j in range(4):
                for a in range(2):
                    kbuf[a, o * 4 + j, pl.ds(s * PART, PART), :] = kv[o * 4 + s][j, a]
    pos_ref[...] = row_positions(part)
    qgrp = query_groups(at, groups)
    stats[...] = jnp.zeros_like(stats)
    for h in range(HEADS):
        cols = slice(h * HD, (h + 1) * HD)

        def step(ks, carry):
            key = kbuf[0, ks, :, cols]
            value = kbuf[1, ks, :, cols]
            group = groups[key_slot(at, ks)]
            live = pos_ref[...] < valid[group]
            out = []
            for n in range(QROWS // QCHUNK):
                rows = slice(n * QCHUNK, (n + 1) * QCHUNK)
                top, total, weighted = carry[n]
                scores = dot(key, qbuf[0, rows, cols], NT)
                dprobs = dot(value, qbuf[1, rows, cols], NT)
                scores = jnp.where(live, scores * (SCALE * LOG2E), NEG)
                ok = qgrp[:, rows] >= group
                new_top = jnp.where(ok, jnp.maximum(top, jnp.max(scores, axis=0, keepdims=True)), top)
                weights = jnp.exp2(scores - jnp.where(ok, new_top, -NEG))
                factor = jnp.exp2(top - new_top)
                total = total * factor + jnp.sum(weights, axis=0, keepdims=True)
                weighted = weighted * factor + jnp.sum(weights * dprobs, axis=0, keepdims=True)
                out.append((new_top, total, weighted))
            return tuple(out)

        start = (
            jnp.full((1, QCHUNK), NEG, jnp.float32),
            jnp.zeros((1, QCHUNK), jnp.float32),
            jnp.zeros((1, QCHUNK), jnp.float32),
        )
        final = lax.fori_loop(0, 8, step, (start,) * (QROWS // QCHUNK))
        for n in range(QROWS // QCHUNK):
            rows = slice(n * QCHUNK, (n + 1) * QCHUNK)
            stats[h : h + 1, rows] = final[n][0]
            stats[3 + h : 4 + h, rows] = final[n][1]
            stats[6 + h : 7 + h, rows] = final[n][2]


def grad_kernel(at, groups, valid, qbuf, kbuf, st0, st1, st2, st3, *refs):
    dq = refs[0:4]
    dkv = refs[4:12]
    pos_ref, log_ref, delta_ref, dqt = refs[12:16]
    pos_ref[...] = row_positions(at[2])
    qgrp = query_groups(at, groups)
    sts = [st0[...]]
    for shift, st in enumerate((st1, st2, st3), 1):
        moved = QROWS - shift * GROUP
        sts.append(jnp.concatenate([st[:, moved:], st[:, :moved]], axis=1))
    tops = [st[0:3, :] for st in sts]
    top = functools.reduce(jnp.maximum, tops)
    factors = [jnp.exp2(t - top) for t in tops]
    total = sum(f * st[3:6, :] for f, st in zip(factors, sts))
    weighted = sum(f * st[6:9, :] for f, st in zip(factors, sts))
    log_ref[0:3, :] = top + jnp.log2(total)
    delta_ref[0:3, :] = weighted / total
    dqt[...] = jnp.zeros_like(dqt)
    for h in range(HEADS):
        cols = slice(h * HD, (h + 1) * HD)
        for o in range(2):

            def step(j, _):
                ks = o * 4 + j
                key = kbuf[0, ks, :, cols]
                value = kbuf[1, ks, :, cols]
                group = groups[key_slot(at, ks)]
                live = pos_ref[...] < valid[group]
                key_grad = jnp.zeros((GROUP, HD), jnp.float32)
                value_grad = jnp.zeros((GROUP, HD), jnp.float32)
                for n in range(QROWS // QCHUNK):
                    rows = slice(n * QCHUNK, (n + 1) * QCHUNK)
                    query = qbuf[0, rows, cols]
                    grad = qbuf[1, rows, cols]
                    scores = dot(key, query, NT)
                    dprobs = dot(value, grad, NT)
                    level = jnp.where(qgrp[:, rows] >= group, log_ref[h : h + 1, rows], -NEG)
                    probs = jnp.exp2(jnp.where(live, scores * (SCALE * LOG2E), NEG) - level)
                    dscores = (probs * (dprobs - delta_ref[h : h + 1, rows])).astype(jnp.bfloat16)
                    value_grad += dot(probs.astype(jnp.bfloat16), grad, NN)
                    key_grad += dot(dscores, query, NN)
                    dqt[h, :, rows] += dot(key, dscores, TN)
                key_grad = (key_grad * SCALE).astype(jnp.bfloat16)
                value_grad = value_grad.astype(jnp.bfloat16)
                for s in range(4):
                    piece = slice(s * PART, (s + 1) * PART)
                    dkv[o * 4 + s][j, 0, :, cols] = key_grad[piece]
                    dkv[o * 4 + s][j, 1, :, cols] = value_grad[piece]
                return 0

            lax.fori_loop(0, 4, step, 0)
        query_grad = (dqt[h] * SCALE).T.astype(jnp.bfloat16)
        for s in range(4):
            for j in range(4):
                first = (s * 4 + j) * PART
                dq[s][j, :, cols] = query_grad[first : first + PART]


SMEM = pl.BlockSpec(memory_space=pltpu.SMEM)
VMEM = pl.BlockSpec(memory_space=pltpu.VMEM)
PARAMS = pltpu.CompilerParams(vmem_limit_bytes=48 * 1024 * 1024)


def local(query, keys, values, dout, slot_group, valid):
    tm = lax.axis_index("tm")
    head = lax.axis_index("head")
    y, z, x, c = tm // NZ, tm % NZ, head // NC, head % NC
    at = jnp.stack([y, z, x, c])
    bf16, f32 = jnp.bfloat16, jnp.float32

    keep, give = pl.pallas_call(
        pack_kernel,
        out_shape=(jax.ShapeDtypeStruct((4, 4, SUB, COLS), bf16),) * 2,
        in_specs=[SMEM] + [VMEM] * 4,
        out_specs=(VMEM,) * 2,
        name="pack",
    )(at, query, dout, keys, values)
    take = swap_core(give)
    both = jnp.where(c == 0, jnp.concatenate([keep, take], axis=2), jnp.concatenate([take, keep], axis=2))
    received = [send(both[j], lambda y, z, x, c: (y, z + c + 2 * j, x, c)) for j in range(4)]
    own_qd = jnp.stack([r[0:2] for r in received])
    own_kv = jnp.stack([r[2:4] for r in received])

    kvs = [own_kv] + [send(own_kv, lambda y, z, x, c: (y, z, x + s, c)) for s in (1, 2, 3)]
    qds = [own_qd] + [send(own_qd, lambda y, z, x, c: (y + s, z, x, c)) for s in (1, 2, 3)]
    kvs = kvs + [swap_core(kv) for kv in kvs]

    qbuf, kbuf, stats = pl.pallas_call(
        stats_kernel,
        out_shape=(
            jax.ShapeDtypeStruct((2, QROWS, COLS), bf16),
            jax.ShapeDtypeStruct((2, 8, GROUP, COLS), bf16),
            jax.ShapeDtypeStruct((16, QROWS), f32),
        ),
        in_specs=[SMEM] * 3 + [VMEM] * 12,
        out_specs=(VMEM,) * 3,
        scratch_shapes=[pltpu.VMEM((GROUP, QCHUNK), jnp.int32)],
        compiler_params=PARAMS,
        name="stats",
    )(at, slot_group, valid, *qds, *kvs)

    all_stats = [stats] + [send(stats, lambda y, z, x, c: (y + s, z, x, c)) for s in (1, 2, 3)]

    outs = pl.pallas_call(
        grad_kernel,
        out_shape=(jax.ShapeDtypeStruct((4, PART, COLS), bf16),) * 4
        + (jax.ShapeDtypeStruct((4, 2, PART, COLS), bf16),) * 8,
        in_specs=[SMEM] * 3 + [VMEM] * 6,
        out_specs=(VMEM,) * 12,
        scratch_shapes=[
            pltpu.VMEM((GROUP, QCHUNK), jnp.int32),
            pltpu.VMEM((8, QROWS), f32),
            pltpu.VMEM((8, QROWS), f32),
            pltpu.VMEM((HEADS, HD, QROWS), f32),
        ],
        compiler_params=PARAMS,
        name="grads",
    )(at, slot_group, valid, qbuf, kbuf, *all_stats)
    dq, dkv_own, dkv_other = outs[0:4], outs[4:8], outs[8:12]

    dq_got = [send(dq[s], lambda y, z, x, c: (y - s, z, x, c)) for s in (1, 2, 3)]
    dkv = [a.astype(f32) + swap_core(b).astype(f32) for a, b in zip(dkv_own, dkv_other)]
    dkv_got = [send(dkv[s].astype(bf16), lambda y, z, x, c: (y, z, x - s, c)) for s in (1, 2, 3)]
    dq_sum = (dq[0].astype(f32) + sum(g.astype(f32) for g in dq_got)).astype(bf16)
    dkv_sum = (dkv[0] + sum(g.astype(f32) for g in dkv_got)).astype(bf16)

    back = []
    for j in range(4):
        block = jnp.concatenate([dq_sum[j][None], dkv_sum[j]], axis=0)
        back.append(send(block, lambda y, z, x, c: (y, z - c - 2 * j, x, c)))
    first = jnp.stack([b[:, :SUB] for b in back])
    second = jnp.stack([b[:, SUB:] for b in back])
    theirs = swap_core(jnp.where(c == 0, second, first))
    return pl.pallas_call(
        unpack_kernel,
        out_shape=(jax.ShapeDtypeStruct((SUB, NZ * COLS), bf16),) * 3,
        in_specs=[SMEM] + [VMEM] * 2,
        out_specs=(VMEM,) * 3,
        name="unpack",
    )(at, jnp.where(c == 0, first, second), theirs)


def solution(mesh):
    spec = P(("tm", "head"), None)
    return jax.shard_map(
        local,
        mesh=mesh,
        in_specs=(spec, spec, spec, spec, P(), P()),
        out_specs=(spec, spec, spec),
        check_vma=False,
    )
```

time: 739 us -> 142 us (0.19)
  local copies, waits for them, and re-layouts: 178 us -> 0.94 us
  other arithmetic: 105 us -> 3.21 us
  matrix products: 93.6 us -> 0 us
  blocking collectives: 93.4 us -> 0 us
  waiting for transfers between devices: 139 us -> 57.4 us
  loops' own time: 68.9 us -> 0 us
  Pallas kernels: 0 us -> 37.7 us
  between operations: 14 us -> 0.91 us
    dynamic_slice x192 -> x0, local copies, waits for them, and re-layouts: 154 us -> none  [in_blocks(): lax.scan(one_block, carry, (jnp.arange(block_count, dtype=jnp.int32), sta...]
    all_gather x4 -> x0, waiting for transfers between devices: 130 us -> none  [the longest x1 83.4 us: local(): lax.all_gather(values, 'tm', axis=0, tiled=True)]
    dot_general x224 -> x0, matrix products: 93.6 us -> none  [the longest x32 18.9 us: keyside_update(): jnp.einsum('hqk,qhd->khd', dscores, piece_query_heads, preferred_element_...]
    another operation x3 -> x0, loops' own time: 68.9 us -> none  [in_blocks(): lax.scan(one_block, carry, (jnp.arange(block_count, dtype=jnp.int32), sta...]
    all_gather x2 -> x0, blocking collectives: 63 us -> none  [the longest x1 32.1 us: local(): lax.all_gather(log_total.T, 'tm', axis=0, tiled=True)]
    ppermute x0 -> x33, waiting for transfers between devices: none -> 57.4 us  [send(): return lax.ppermute(array, ('tm', 'head'), pairs(move))]
    ppermute x0 -> x33, starting transfers between devices: none -> 41.6 us  [send(): return lax.ppermute(array, ('tm', 'head'), pairs(move))]
    all_to_all x4 -> x0, starting transfers between devices: 41.2 us -> none  [the longest x1 24.9 us: local(): lax.all_to_all(key_out, 'head', split_axis=0, concat_axis=1, tiled=True)]
  transfers between devices with their start and end apart: 8 -> 33, of which waited for: 5 -> 20; matrix products, arithmetic and copies ran while one was open for 51% -> 0% of each run, Pallas kernels for 0% -> 0%
where the time goes in v1:
time: 142 us
  waiting for transfers between devices  57.4 us (40%)
  starting transfers between devices  41.6 us (29%)
  Pallas kernels  37.7 us (27%)
  other arithmetic  3.21 us (2%)
    ppermute x33, waiting for transfers between devices, send(): return lax.ppermute(array, ('tm', 'head'), pairs(move))  57.4 us
    ppermute x33, starting transfers between devices, send(): return lax.ppermute(array, ('tm', 'head'), pairs(move))  41.6 us
    pallas_call x1, Pallas kernels, local(): pl.pallas_call(grad_kernel, out_shape=(jax.ShapeDtypeStruct((4, PART, COL...  21.9 us
    pallas_call x1, Pallas kernels, local(): pl.pallas_call(stats_kernel, out_shape=(jax.ShapeDtypeStruct((2, QROWS, C...  11.9 us
  transfers between devices with their start and end apart: 33, of which 20 were waited for; matrix products, arithmetic and copies ran while one was open for 0% of the time, Pallas kernels for 0%

profile of v1, /device:TPU:1, one launch (start us, length us, event | category | flops | bytes accessed | tf_op | source)
XLA Modules:
  0.0 141.9 jit_solution(7416043298225279026)
XLA Ops:
  1.2 2.0 %pack.1 = (bf16[4,4,24,384]{3,2,1,0:T(8,128)(2,1)}, bf16[4,4,24,384]{3,2,1,0:T(8,128)(2,1)}) custom-call(s32[4]{0:T(128)} %pad_add_fusion.at, bf16[24,3072]{1,0:T(8,128)(2,1)} %query.1, bf16[24,3072]{1,0:T(8,128)(2,1)} %grad.1, bf16[24,3072]{1,0:T(8,128)(2,1)} %keys.1, bf16[24,3072]{1,0:T(8,128)(2,1)} %values.1), custom_call_target="tpu_custom_call" | custom-call | tf_op jit(solution)/shard_map/pack/pallas_call | solution.py:226
  3.2 3.2 %collective-permute-start = (bf16[4,4,24,384]{3,2,1,0:T(8,128)(2,1)}, bf16[4,4,24,384]{3,2,1,0:T(8,128)(2,1)S(1)}, u32[]{:S(2)}, u32[]{:S(2)}) collective-permute-start(bf16[4,4,24,384]{3,2,1,0:T(8,128)(2,1)} %get-tuple-element.21), channel_id=1, source_target_pairs={{0,1},{1,0},{2,3},{3,2},{4,5},{5,4},{6,7},{7,6},{8,9},{9,8},{10,11... | collective-permute-start | bytes 884744 | tf_op jit(solution)/shard_map/ppermute | solution.py:42
  9.2 1.9 %collective-permute-start.1 = (bf16[4,48,384]{2,1,0:T(8,128)(2,1)S(1)}, bf16[4,48,384]{2,1,0:T(8,128)(2,1)S(1)}, u32[]{:S(2)}, u32[]{:S(2)}) collective-permute-start(bf16[4,48,384]{2,1,0:T(8,128)(2,1)S(1)} %get-tuple-element.37), channel_id=1, source_target_pairs={{0,0},{1,9},{2,2},{3,11},{4,4},{5,13},{6,6},{7,15},{8,8},{9,17},{1... | collective-permute-start | bytes 442376 | tf_op jit(solution)/shard_map/ppermute | solution.py:42
  11.1 3.9 %collective-permute-start.4 = (bf16[4,48,384]{2,1,0:T(8,128)(2,1)S(1)}, bf16[4,48,384]{2,1,0:T(8,128)(2,1)S(1)}, u32[]{:S(2)}, u32[]{:S(2)}) collective-permute-start(bf16[4,48,384]{2,1,0:T(8,128)(2,1)S(1)} %get-tuple-element.38), channel_id=1, source_target_pairs={{0,48},{1,57},{2,50},{3,59},{4,52},{5,61},{6,54},{7,63},{8,56},{9,... | collective-permute-start | bytes 442376 | tf_op jit(solution)/shard_map/ppermute | solution.py:42
  15.0 2.3 %collective-permute-start.3 = (bf16[4,48,384]{2,1,0:T(8,128)(2,1)S(1)}, bf16[4,48,384]{2,1,0:T(8,128)(2,1)S(1)}, u32[]{:S(2)}, u32[]{:S(2)}) collective-permute-start(bf16[4,48,384]{2,1,0:T(8,128)(2,1)S(1)} %get-tuple-element.39), channel_id=1, source_target_pairs={{0,32},{1,41},{2,34},{3,43},{4,36},{5,45},{6,38},{7,47},{8,40},{9,... | collective-permute-start | bytes 442376 | tf_op jit(solution)/shard_map/ppermute | solution.py:42
  18.3 5.1 %collective-permute-done.4 = bf16[4,48,384]{2,1,0:T(8,128)(2,1)S(1)} collective-permute-done((bf16[4,48,384]{2,1,0:T(8,128)(2,1)S(1)}, bf16[4,48,384]{2,1,0:T(8,128)(2,1)S(1)}, u32[]{:S(2)}, u32[]{:S(2)}) %collective-permute-start.4) | collective-permute-done | bytes 147488 | tf_op jit(solution)/shard_map/ppermute | solution.py:42
  23.5 4.7 %collective-permute-done.3 = bf16[4,48,384]{2,1,0:T(8,128)(2,1)S(1)} collective-permute-done((bf16[4,48,384]{2,1,0:T(8,128)(2,1)S(1)}, bf16[4,48,384]{2,1,0:T(8,128)(2,1)S(1)}, u32[]{:S(2)}, u32[]{:S(2)}) %collective-permute-start.3) | collective-permute-done | bytes 147488 | tf_op jit(solution)/shard_map/ppermute | solution.py:42
  28.2 2.3 %collective-permute-done.2 = bf16[4,48,384]{2,1,0:T(8,128)(2,1)S(1)} collective-permute-done((bf16[4,48,384]{2,1,0:T(8,128)(2,1)S(1)}, bf16[4,48,384]{2,1,0:T(8,128)(2,1)S(1)}, u32[]{:S(2)}, u32[]{:S(2)}) %collective-permute-start.2) | collective-permute-done | bytes 147488 | tf_op jit(solution)/shard_map/ppermute | solution.py:42
  30.6 2.9 %collective-permute-start.7 = (bf16[4,2,48,384]{3,2,1,0:T(8,128)(2,1)S(1)}, bf16[4,2,48,384]{3,2,1,0:T(8,128)(2,1)S(1)}, u32[]{:S(2)}, u32[]{:S(2)}) collective-permute-start(bf16[4,2,48,384]{3,2,1,0:T(8,128)(2,1)S(1)} %pad_maximum_fusion.refs_0_), channel_id=1, source_target_pairs={{0,192},{1,193},{2,194},{3,195},{4,196},{5,197},{6,198},{7,199},{8... | collective-permute-start | bytes 884744 | tf_op jit(solution)/shard_map/ppermute | solution.py:42
  33.8 2.6 %collective-permute-start.10 = (bf16[4,2,48,384]{3,2,1,0:T(8,128)(2,1)S(1)}, bf16[4,2,48,384]{3,2,1,0:T(8,128)(2,1)S(1)}, u32[]{:S(2)}, u32[]{:S(2)}) collective-permute-start(bf16[4,2,48,384]{3,2,1,0:T(8,128)(2,1)S(1)} %pad_maximum_fusion.1.refs_4_), channel_id=1, source_target_pairs={{0,6},{1,7},{2,0},{3,1},{4,2},{5,3},{6,4},{7,5},{8,14},{9,15},{10,... | collective-permute-start | bytes 884744 | tf_op jit(solution)/shard_map/ppermute | solution.py:42
  37.5 7.5 %collective-permute-done.7.refs_3_ = bf16[4,2,48,384]{3,2,1,0:T(8,128)(2,1)S(1)} collective-permute-done((bf16[4,2,48,384]{3,2,1,0:T(8,128)(2,1)S(1)}, bf16[4,2,48,384]{3,2,1,0:T(8,128)(2,1)S(1)}, u32[]{:S(2)}, u32[]{:S(2)}) %collective-permute-start.7) | collective-permute-done | bytes 294944 | tf_op jit(solution)/shard_map/ppermute | solution.py:42
  45.0 3.5 %collective-permute-done.10.refs_7_ = bf16[4,2,48,384]{3,2,1,0:T(8,128)(2,1)S(1)} collective-permute-done((bf16[4,2,48,384]{3,2,1,0:T(8,128)(2,1)S(1)}, bf16[4,2,48,384]{3,2,1,0:T(8,128)(2,1)S(1)}, u32[]{:S(2)}, u32[]{:S(2)}) %collective-permute-start.10) | collective-permute-done | bytes 294944 | tf_op jit(solution)/shard_map/ppermute | solution.py:42
  49.0 3.4 %collective-permute-done.8.refs_5_ = bf16[4,2,48,384]{3,2,1,0:T(8,128)(2,1)S(1)} collective-permute-done((bf16[4,2,48,384]{3,2,1,0:T(8,128)(2,1)S(1)}, bf16[4,2,48,384]{3,2,1,0:T(8,128)(2,1)S(1)}, u32[]{:S(2)}, u32[]{:S(2)}) %collective-permute-start.8) | collective-permute-done | bytes 294944 | tf_op jit(solution)/shard_map/ppermute | solution.py:42
  54.0 11.9 %stats.1 = (bf16[2,768,384]{2,1,0:T(8,128)(2,1)S(1)}, bf16[2,8,192,384]{3,2,1,0:T(8,128)(2,1)}, f32[16,768]{1,0:T(8,128)S(1)}) custom-call(s32[4]{0:T(128)S(1)} %copy-done, s32[32]{0:T(128)S(1)} %copy-done.1, s32[32]{0:T(128)S(1)} %copy-done.2, bf16[4,2,48,384]{3,2,1,0:T(8,128)(2,1)S(1)} %pad_maximum_fusion.refs_0_, ...), custom_call_target="tpu_custom_call" | custom-call | tf_op jit(solution)/shard_map/stats/pallas_call | solution.py:243
  66.8 1.9 %collective-permute-start.16 = (f32[16,768]{1,0:T(8,128)S(1)}, f32[16,768]{1,0:T(8,128)S(1)}, u32[]{:S(2)}, u32[]{:S(2)}) collective-permute-start(f32[16,768]{1,0:T(8,128)S(1)} %get-tuple-element.24.st0), channel_id=1, source_target_pairs={{0,128},{1,129},{2,130},{3,131},{4,132},{5,133},{6,134},{7,135},{8... | collective-permute-start | bytes 147464 | tf_op jit(solution)/shard_map/ppermute | solution.py:42
  71.2 1.8 %collective-permute-done.15.st1 = f32[16,768]{1,0:T(8,128)S(1)} collective-permute-done((f32[16,768]{1,0:T(8,128)S(1)}, f32[16,768]{1,0:T(8,128)S(1)}, u32[]{:S(2)}, u32[]{:S(2)}) %collective-permute-start.15) | collective-permute-done | bytes 49184 | tf_op jit(solution)/shard_map/ppermute | solution.py:42
  73.0 21.9 %grads.1 = (bf16[4,48,384]{2,1,0:T(8,128)(2,1)S(1)}, bf16[4,48,384]{2,1,0:T(8,128)(2,1)S(1)}, bf16[4,48,384]{2,1,0:T(8,128)(2,1)S(1)}, bf16[4,48,384]{2,1,0:T(8,...) custom-call(s32[4]{0:T(128)S(1)} %copy-done, ...), custom_call_target="tpu_custom_call" | custom-call | tf_op jit(solution)/shard_map/grads/pallas_call | solution.py:259
  94.9 1.8 %collective-permute-start.22 = (bf16[4,2,48,384]{3,2,1,0:T(8,128)(2,1)S(1)}, bf16[4,2,48,384]{3,2,1,0:T(8,128)(2,1)S(1)}, u32[]{:S(2)}, u32[]{:S(2)}) collective-permute-start(bf16[4,2,48,384]{3,2,1,0:T(8,128)(2,1)S(1)} %get-tuple-element.32), channel_id=1, source_target_pairs={{0,1},{1,0},{2,3},{3,2},{4,5},{5,4},{6,7},{7,6},{8,9},{9,8},{10,11... | collective-permute-start | bytes 884744 | tf_op jit(solution)/shard_map/ppermute | solution.py:42
  103.5 4.2 %collective-permute-done.20 = bf16[4,48,384]{2,1,0:T(8,128)(2,1)S(1)} collective-permute-done((bf16[4,48,384]{2,1,0:T(8,128)(2,1)S(1)}, bf16[4,48,384]{2,1,0:T(8,128)(2,1)S(1)}, u32[]{:S(2)}, u32[]{:S(2)}) %collective-permute-start.20) | collective-permute-done | bytes 147488 | tf_op jit(solution)/shard_map/ppermute | solution.py:42
  109.8 8.4 %collective-permute-done.27 = bf16[4,2,48,384]{3,2,1,0:T(8,128)(2,1)S(1)} collective-permute-done((bf16[4,2,48,384]{3,2,1,0:T(8,128)(2,1)S(1)}, bf16[4,2,48,384]{3,2,1,0:T(8,128)(2,1)S(1)}, u32[]{:S(2)}, u32[]{:S(2)}) %collective-permute-start.27) | collective-permute-done | bytes 294944 | tf_op jit(solution)/shard_map/ppermute | solution.py:42
  118.5 7.9 %collective-permute-start.29 = (bf16[3,48,384]{2,1,0:T(8,128)(2,1)S(1)}, bf16[3,48,384]{2,1,0:T(8,128)(2,1)S(1)}, u32[]{:S(2)}, u32[]{:S(2)}) collective-permute-start(bf16[3,48,384]{2,1,0:T(8,128)(2,1)S(1)} %pad_maximum_fusion.5), channel_id=1, source_target_pairs={{0,48},{1,41},{2,50},{3,43},{4,52},{5,45},{6,54},{7,47},{8,56},{9,... | collective-permute-start | bytes 331784 | tf_op jit(solution)/shard_map/ppermute | solution.py:42
  126.6 4.6 %collective-permute-start.28 = (bf16[3,48,384]{2,1,0:T(8,128)(2,1)S(1)}, bf16[3,48,384]{2,1,0:T(8,128)(2,1)S(1)}, u32[]{:S(2)}, u32[]{:S(2)}) collective-permute-start(bf16[3,48,384]{2,1,0:T(8,128)(2,1)S(1)} %pad_maximum_fusion.4), channel_id=1, source_target_pairs={{0,0},{1,57},{2,2},{3,59},{4,4},{5,61},{6,6},{7,63},{8,8},{9,1},{1... | collective-permute-start | bytes 331784 | tf_op jit(solution)/shard_map/ppermute | solution.py:42
  131.5 5.4 %collective-permute-done.30 = bf16[3,48,384]{2,1,0:T(8,128)(2,1)S(1)} collective-permute-done((bf16[3,48,384]{2,1,0:T(8,128)(2,1)S(1)}, bf16[3,48,384]{2,1,0:T(8,128)(2,1)S(1)}, u32[]{:S(2)}, u32[]{:S(2)}) %collective-permute-start.30) | collective-permute-done | bytes 110624 | tf_op jit(solution)/shard_map/ppermute | solution.py:42
  140.0 1.9 %unpack.1 = (bf16[24,3072]{1,0:T(8,128)(2,1)}, bf16[24,3072]{1,0:T(8,128)(2,1)}, bf16[24,3072]{1,0:T(8,128)(2,1)}) custom-call(s32[4]{0:T(128)} %pad_add_fusion.at, bf16[4,3,24,384]{3,2,1,0:T(8,128)(2,1)} %get-tuple-element.42.mine, bf16[4,3,24,384]{3,2,1,0:T(8,128)(2,1)} %copy-done.3), custom_call_target="tpu_custom_call" | custom-call | tf_op jit(solution)/shard_map/unpack/pallas_call | solution.py:289
  (79 shorter events, 23.9 us)
Async XLA Ops:
  3.2 4.7 %collective-permute-start = (bf16[4,4,24,384]{3,2,1,0:T(8,128)(2,1)}, bf16[4,4,24,384]{3,2,1,0:T(8,128)(2,1)S(1)}, u32[]{:S(2)}, u32[]{:S(2)}) collective-permute-start(bf16[4,4,24,384]{3,2,1,0:T(8,128)(2,1)} %get-tuple-element.21), channel_id=1, source_target_pairs={{0,1},{1,0},{2,3},{3,2},{4,5},{5,4},{6,7},{7,6},{8,9},{9,8},{10,11... | collective-permute-start | bytes 884744 | tf_op jit(solution)/shard_map/ppermute | solution.py:42
  9.2 9.1 %collective-permute-start.1 = (bf16[4,48,384]{2,1,0:T(8,128)(2,1)S(1)}, bf16[4,48,384]{2,1,0:T(8,128)(2,1)S(1)}, u32[]{:S(2)}, u32[]{:S(2)}) collective-permute-start(bf16[4,48,384]{2,1,0:T(8,128)(2,1)S(1)} %get-tuple-element.37), channel_id=1, source_target_pairs={{0,0},{1,9},{2,2},{3,11},{4,4},{5,13},{6,6},{7,15},{8,8},{9,17},{1... | collective-permute-start | bytes 442376 | tf_op jit(solution)/shard_map/ppermute | solution.py:42
  11.1 12.3 %collective-permute-start.4 = (bf16[4,48,384]{2,1,0:T(8,128)(2,1)S(1)}, bf16[4,48,384]{2,1,0:T(8,128)(2,1)S(1)}, u32[]{:S(2)}, u32[]{:S(2)}) collective-permute-start(bf16[4,48,384]{2,1,0:T(8,128)(2,1)S(1)} %get-tuple-element.38), channel_id=1, source_target_pairs={{0,48},{1,57},{2,50},{3,59},{4,52},{5,61},{6,54},{7,63},{8,56},{9,... | collective-permute-start | bytes 442376 | tf_op jit(solution)/shard_map/ppermute | solution.py:42
  15.0 13.1 %collective-permute-start.3 = (bf16[4,48,384]{2,1,0:T(8,128)(2,1)S(1)}, bf16[4,48,384]{2,1,0:T(8,128)(2,1)S(1)}, u32[]{:S(2)}, u32[]{:S(2)}) collective-permute-start(bf16[4,48,384]{2,1,0:T(8,128)(2,1)S(1)} %get-tuple-element.39), channel_id=1, source_target_pairs={{0,32},{1,41},{2,34},{3,43},{4,36},{5,45},{6,38},{7,47},{8,40},{9,... | collective-permute-start | bytes 442376 | tf_op jit(solution)/shard_map/ppermute | solution.py:42
  17.4 13.1 %collective-permute-start.2 = (bf16[4,48,384]{2,1,0:T(8,128)(2,1)S(1)}, bf16[4,48,384]{2,1,0:T(8,128)(2,1)S(1)}, u32[]{:S(2)}, u32[]{:S(2)}) collective-permute-start(bf16[4,48,384]{2,1,0:T(8,128)(2,1)S(1)} %get-tuple-element.40), channel_id=1, source_target_pairs={{0,16},{1,25},{2,18},{3,27},{4,20},{5,29},{6,22},{7,31},{8,24},{9,... | collective-permute-start | bytes 442376 | tf_op jit(solution)/shard_map/ppermute | solution.py:42
  30.6 14.4 %collective-permute-start.7 = (bf16[4,2,48,384]{3,2,1,0:T(8,128)(2,1)S(1)}, bf16[4,2,48,384]{3,2,1,0:T(8,128)(2,1)S(1)}, u32[]{:S(2)}, u32[]{:S(2)}) collective-permute-start(bf16[4,2,48,384]{3,2,1,0:T(8,128)(2,1)S(1)} %pad_maximum_fusion.refs_0_), channel_id=1, source_target_pairs={{0,192},{1,193},{2,194},{3,195},{4,196},{5,197},{6,198},{7,199},{8... | collective-permute-start | bytes 884744 | tf_op jit(solution)/shard_map/ppermute | solution.py:42
  33.4 11.5 %collective-permute-start.6 = (bf16[4,2,48,384]{3,2,1,0:T(8,128)(2,1)S(1)}, bf16[4,2,48,384]{3,2,1,0:T(8,128)(2,1)S(1)}, u32[]{:S(2)}, u32[]{:S(2)}) collective-permute-start(bf16[4,2,48,384]{3,2,1,0:T(8,128)(2,1)S(1)} %pad_maximum_fusion.refs_0_), channel_id=1, source_target_pairs={{0,128},{1,129},{2,130},{3,131},{4,132},{5,133},{6,134},{7,135},{8... | collective-permute-start | bytes 884744 | tf_op jit(solution)/shard_map/ppermute | solution.py:42
  33.8 14.7 %collective-permute-start.10 = (bf16[4,2,48,384]{3,2,1,0:T(8,128)(2,1)S(1)}, bf16[4,2,48,384]{3,2,1,0:T(8,128)(2,1)S(1)}, u32[]{:S(2)}, u32[]{:S(2)}) collective-permute-start(bf16[4,2,48,384]{3,2,1,0:T(8,128)(2,1)S(1)} %pad_maximum_fusion.1.refs_4_), channel_id=1, source_target_pairs={{0,6},{1,7},{2,0},{3,1},{4,2},{5,3},{6,4},{7,5},{8,14},{9,15},{10,... | collective-permute-start | bytes 884744 | tf_op jit(solution)/shard_map/ppermute | solution.py:42
  36.4 12.1 %collective-permute-start.9 = (bf16[4,2,48,384]{3,2,1,0:T(8,128)(2,1)S(1)}, bf16[4,2,48,384]{3,2,1,0:T(8,128)(2,1)S(1)}, u32[]{:S(2)}, u32[]{:S(2)}) collective-permute-start(bf16[4,2,48,384]{3,2,1,0:T(8,128)(2,1)S(1)} %pad_maximum_fusion.1.refs_4_), channel_id=1, source_target_pairs={{0,4},{1,5},{2,6},{3,7},{4,0},{5,1},{6,2},{7,3},{8,12},{9,13},{10,... | collective-permute-start | bytes 884744 | tf_op jit(solution)/shard_map/ppermute | solution.py:42
  36.9 15.5 %collective-permute-start.8 = (bf16[4,2,48,384]{3,2,1,0:T(8,128)(2,1)S(1)}, bf16[4,2,48,384]{3,2,1,0:T(8,128)(2,1)S(1)}, u32[]{:S(2)}, u32[]{:S(2)}) collective-permute-start(bf16[4,2,48,384]{3,2,1,0:T(8,128)(2,1)S(1)} %pad_maximum_fusion.1.refs_4_), channel_id=1, source_target_pairs={{0,2},{1,3},{2,4},{3,5},{4,6},{5,7},{6,0},{7,1},{8,10},{9,11},{10,... | collective-permute-start | bytes 884744 | tf_op jit(solution)/shard_map/ppermute | solution.py:42
  45.0 7.9 %collective-permute-start.5 = (bf16[4,2,48,384]{3,2,1,0:T(8,128)(2,1)S(1)}, bf16[4,2,48,384]{3,2,1,0:T(8,128)(2,1)S(1)}, u32[]{:S(2)}, u32[]{:S(2)}) collective-permute-start(bf16[4,2,48,384]{3,2,1,0:T(8,128)(2,1)S(1)} %pad_maximum_fusion.refs_0_), channel_id=1, source_target_pairs={{0,64},{1,65},{2,66},{3,67},{4,68},{5,69},{6,70},{7,71},{8,72},{9,... | collective-permute-start | bytes 884744 | tf_op jit(solution)/shard_map/ppermute | solution.py:42
  45.0 7.9 %collective-permute-start.11 = (bf16[4,2,48,384]{3,2,1,0:T(8,128)(2,1)S(1)}, bf16[4,2,48,384]{3,2,1,0:T(8,128)(2,1)S(1)}, u32[]{:S(2)}, u32[]{:S(2)}) collective-permute-start(bf16[4,2,48,384]{3,2,1,0:T(8,128)(2,1)S(1)} %pad_maximum_fusion.1.refs_4_), channel_id=1, source_target_pairs={{0,1},{1,0},{2,3},{3,2},{4,5},{5,4},{6,7},{7,6},{8,9},{9,8},{10,11... | collective-permute-start | bytes 884744 | tf_op jit(solution)/shard_map/ppermute | solution.py:42
  66.8 4.4 %collective-permute-start.16 = (f32[16,768]{1,0:T(8,128)S(1)}, f32[16,768]{1,0:T(8,128)S(1)}, u32[]{:S(2)}, u32[]{:S(2)}) collective-permute-start(f32[16,768]{1,0:T(8,128)S(1)} %get-tuple-element.24.st0), channel_id=1, source_target_pairs={{0,128},{1,129},{2,130},{3,131},{4,132},{5,133},{6,134},{7,135},{8... | collective-permute-start | bytes 147464 | tf_op jit(solution)/shard_map/ppermute | solution.py:42
  96.8 5.0 %collective-permute-start.18 = (bf16[4,48,384]{2,1,0:T(8,128)(2,1)S(1)}, bf16[4,48,384]{2,1,0:T(8,128)(2,1)S(1)}, u32[]{:S(2)}, u32[]{:S(2)}) collective-permute-start(bf16[4,48,384]{2,1,0:T(8,128)(2,1)S(1)} %get-tuple-element.26), channel_id=1, source_target_pairs={{0,192},{1,193},{2,194},{3,195},{4,196},{5,197},{6,198},{7,199},{8... | collective-permute-start | bytes 442376 | tf_op jit(solution)/shard_map/ppermute | solution.py:42
  97.3 6.2 %collective-permute-start.19 = (bf16[4,48,384]{2,1,0:T(8,128)(2,1)S(1)}, bf16[4,48,384]{2,1,0:T(8,128)(2,1)S(1)}, u32[]{:S(2)}, u32[]{:S(2)}) collective-permute-start(bf16[4,48,384]{2,1,0:T(8,128)(2,1)S(1)} %get-tuple-element.27), channel_id=1, source_target_pairs={{0,128},{1,129},{2,130},{3,131},{4,132},{5,133},{6,134},{7,135},{8... | collective-permute-start | bytes 442376 | tf_op jit(solution)/shard_map/ppermute | solution.py:42
  98.4 9.3 %collective-permute-start.20 = (bf16[4,48,384]{2,1,0:T(8,128)(2,1)S(1)}, bf16[4,48,384]{2,1,0:T(8,128)(2,1)S(1)}, u32[]{:S(2)}, u32[]{:S(2)}) collective-permute-start(bf16[4,48,384]{2,1,0:T(8,128)(2,1)S(1)} %get-tuple-element.28), channel_id=1, source_target_pairs={{0,64},{1,65},{2,66},{3,67},{4,68},{5,69},{6,70},{7,71},{8,72},{9,... | collective-permute-start | bytes 442376 | tf_op jit(solution)/shard_map/ppermute | solution.py:42
  99.6 8.2 %collective-permute-start.21 = (bf16[4,2,48,384]{3,2,1,0:T(8,128)(2,1)S(1)}, bf16[4,2,48,384]{3,2,1,0:T(8,128)(2,1)S(1)}, u32[]{:S(2)}, u32[]{:S(2)}) collective-permute-start(bf16[4,2,48,384]{3,2,1,0:T(8,128)(2,1)S(1)} %get-tuple-element.30), channel_id=1, source_target_pairs={{0,1},{1,0},{2,3},{3,2},{4,5},{5,4},{6,7},{7,6},{8,9},{9,8},{10,11... | collective-permute-start | bytes 884744 | tf_op jit(solution)/shard_map/ppermute | solution.py:42
  100.7 8.2 %collective-permute-start.23 = (bf16[4,2,48,384]{3,2,1,0:T(8,128)(2,1)S(1)}, bf16[4,2,48,384]{3,2,1,0:T(8,128)(2,1)S(1)}, u32[]{:S(2)}, u32[]{:S(2)}) collective-permute-start(bf16[4,2,48,384]{3,2,1,0:T(8,128)(2,1)S(1)} %add_convert_fusion.3), channel_id=1, source_target_pairs={{0,6},{1,7},{2,0},{3,1},{4,2},{5,3},{6,4},{7,5},{8,14},{9,15},{10,... | collective-permute-start | bytes 884744 | tf_op jit(solution)/shard_map/ppermute | solution.py:42
  101.8 8.0 %collective-permute-start.25 = (bf16[4,2,48,384]{3,2,1,0:T(8,128)(2,1)S(1)}, bf16[4,2,48,384]{3,2,1,0:T(8,128)(2,1)S(1)}, u32[]{:S(2)}, u32[]{:S(2)}) collective-permute-start(bf16[4,2,48,384]{3,2,1,0:T(8,128)(2,1)S(1)} %add_convert_fusion.2), channel_id=1, source_target_pairs={{0,4},{1,5},{2,6},{3,7},{4,0},{5,1},{6,2},{7,3},{8,12},{9,13},{10,... | collective-permute-start | bytes 884744 | tf_op jit(solution)/shard_map/ppermute | solution.py:42
  103.5 14.7 %collective-permute-start.27 = (bf16[4,2,48,384]{3,2,1,0:T(8,128)(2,1)S(1)}, bf16[4,2,48,384]{3,2,1,0:T(8,128)(2,1)S(1)}, u32[]{:S(2)}, u32[]{:S(2)}) collective-permute-start(bf16[4,2,48,384]{3,2,1,0:T(8,128)(2,1)S(1)} %add_convert_fusion.1), channel_id=1, source_target_pairs={{0,2},{1,3},{2,4},{3,5},{4,6},{5,7},{6,0},{7,1},{8,10},{9,11},{10,... | collective-permute-start | bytes 884744 | tf_op jit(solution)/shard_map/ppermute | solution.py:42
  118.5 13.1 %collective-permute-start.29 = (bf16[3,48,384]{2,1,0:T(8,128)(2,1)S(1)}, bf16[3,48,384]{2,1,0:T(8,128)(2,1)S(1)}, u32[]{:S(2)}, u32[]{:S(2)}) collective-permute-start(bf16[3,48,384]{2,1,0:T(8,128)(2,1)S(1)} %pad_maximum_fusion.5), channel_id=1, source_target_pairs={{0,48},{1,41},{2,50},{3,43},{4,52},{5,45},{6,54},{7,47},{8,56},{9,... | collective-permute-start | bytes 331784 | tf_op jit(solution)/shard_map/ppermute | solution.py:42
  126.4 10.5 %collective-permute-start.30 = (bf16[3,48,384]{2,1,0:T(8,128)(2,1)S(1)}, bf16[3,48,384]{2,1,0:T(8,128)(2,1)S(1)}, u32[]{:S(2)}, u32[]{:S(2)}) collective-permute-start(bf16[3,48,384]{2,1,0:T(8,128)(2,1)S(1)} %pad_maximum_fusion.6), channel_id=1, source_target_pairs={{0,32},{1,25},{2,34},{3,27},{4,36},{5,29},{6,38},{7,31},{8,40},{9,... | collective-permute-start | bytes 331784 | tf_op jit(solution)/shard_map/ppermute | solution.py:42
  126.5 10.4 %collective-permute-start.31 = (bf16[3,48,384]{2,1,0:T(8,128)(2,1)S(1)}, bf16[3,48,384]{2,1,0:T(8,128)(2,1)S(1)}, u32[]{:S(2)}, u32[]{:S(2)}) collective-permute-start(bf16[3,48,384]{2,1,0:T(8,128)(2,1)S(1)} %pad_maximum_fusion.7), channel_id=1, source_target_pairs={{0,16},{1,9},{2,18},{3,11},{4,20},{5,13},{6,22},{7,15},{8,24},{9,1... | collective-permute-start | bytes 331784 | tf_op jit(solution)/shard_map/ppermute | solution.py:42
  126.6 10.4 %collective-permute-start.28 = (bf16[3,48,384]{2,1,0:T(8,128)(2,1)S(1)}, bf16[3,48,384]{2,1,0:T(8,128)(2,1)S(1)}, u32[]{:S(2)}, u32[]{:S(2)}) collective-permute-start(bf16[3,48,384]{2,1,0:T(8,128)(2,1)S(1)} %pad_maximum_fusion.4), channel_id=1, source_target_pairs={{0,0},{1,57},{2,2},{3,59},{4,4},{5,61},{6,6},{7,63},{8,8},{9,1},{1... | collective-permute-start | bytes 331784 | tf_op jit(solution)/shard_map/ppermute | solution.py:42
  (13 other events, 139.0 us)
